TPU v7x, 128 devices: a whole 4x4x4 slice. The times are simulated.
128 devices in a mesh: col: 8 (over y, core), row: 16 (over z, x).
Axes of the slice: x: 4, y: 4, z: 4, core: 2. Of those that a mesh axis runs over, the one named last changes fastest.
Arguments:
- snapshots: float32 [65536, 2048], P('row', 'col'), may hold values from -80 to 80
- orientation: int32 [2, 8], replicated, may hold values from 0 to 1
Outputs:
- rotated: float32 [65536, 2048], P('row', 'col')
- basis: float32 [2048, 2048], P('row', 'col')
All inputs are finite; a program needn't handle non-finite values.
Results may differ from a plain program's by a relative error of at most 0.00065.
Values sent between devices are 32-bit elements; how exact they have to be, the bound alone decides.
A program may use at most 64 MiB of HBM per device.

v0:
```python
import jax
import jax.numpy as jnp
from jax import lax
from jax.sharding import PartitionSpec as P

STEPS = 24


def shifted(value, axis, by):
    size = lax.axis_size(axis)
    pairs = [(i, i + by) for i in range(size) if 0 <= i + by < size]
    return lax.ppermute(value, axis, pairs)


def turn_columns(matrix, cosine, sine_value):
    half_width = cosine.shape[0]
    left_half = matrix[:, :half_width]
    right_half = matrix[:, half_width:]
    first_part = left_half * cosine[None, :] - right_half * sine_value[None, :]
    second_part = left_half * sine_value[None, :] + right_half * cosine[None, :]
    return jnp.concatenate(
        [
            first_part[:, :1],
            second_part[:, :1],
            first_part[:, 1 : half_width - 1],
            second_part[:, 1:],
            first_part[:, half_width - 1 :],
        ],
        1,
    )


def jacobi_steps(gram_matrix, step_count):
    half_width = gram_matrix.shape[0] // 2

    def rotation_step(step_index, loop_state):
        current, rotation = loop_state
        first_diag = jnp.diagonal(current[:half_width, :half_width])
        second_diag = jnp.diagonal(current[half_width:, half_width:])
        coupling = jnp.diagonal(current[:half_width, half_width:])
        spread = second_diag - first_diag
        orient_sign = jnp.where(spread >= 0.0, 1.0, -1.0).astype(jnp.float32)
        tangent = (
            orient_sign
            * 2.0
            * coupling
            / (jnp.abs(spread) + jnp.sqrt(spread * spread + 4.0 * coupling * coupling))
        )
        cosine = 1.0 / jnp.sqrt(1.0 + tangent * tangent)
        sine_value = tangent * cosine
        right_side = turn_columns(current, cosine, sine_value)
        current = turn_columns(right_side.T, cosine, sine_value).T
        rotation = turn_columns(rotation, cosine, sine_value)
        return (current, rotation)

    start = jnp.eye(2 * half_width, dtype=jnp.float32)
    return lax.fori_loop(0, step_count, rotation_step, (gram_matrix, start))


def swap_pair(flipped, first_item, second_item):
    return (
        jnp.where(flipped, second_item, first_item),
        jnp.where(flipped, first_item, second_item),
    )


def whole_gram(upper_block, lower_block):
    joined = jnp.concatenate([upper_block, lower_block], 1)
    local_gram = lax.dot_general(
        joined,
        joined,
        (((0,), (0,)), ((), ())),
        precision=lax.Precision.HIGHEST,
        preferred_element_type=jnp.float32,
    )
    return lax.psum(local_gram, "row")


def on_device(snapshots, orientation):
    block_width = snapshots.shape[1] // 2
    col_index = lax.axis_index("col")
    groups = lax.axis_size("col")
    basis_rows = 2 * block_width * groups // lax.axis_size("row")
    row_ids = lax.axis_index("row") * basis_rows + jnp.arange(basis_rows, dtype=jnp.int32)
    col_ids = col_index * 2 * block_width + jnp.arange(2 * block_width, dtype=jnp.int32)
    basis_pair = (row_ids[:, None] == col_ids[None, :]).astype(jnp.float32)
    upper_block = snapshots[:, :block_width]
    lower_block = snapshots[:, block_width:]
    upper_basis = basis_pair[:, :block_width]
    lower_basis = basis_pair[:, block_width:]
    total_rounds = orientation.shape[0]
    at_start = col_index == 0
    at_end = col_index == groups - 1
    for round_index in range(total_rounds):
        flag_value = lax.dynamic_index_in_dim(
            orientation[round_index], col_index, 0, keepdims=False
        )
        flipped = flag_value == 1
        upper_block, lower_block = swap_pair(flipped, upper_block, lower_block)
        upper_basis, lower_basis = swap_pair(flipped, upper_basis, lower_basis)
        gram_matrix = whole_gram(upper_block, lower_block)
        final_gram, rotation = jacobi_steps(gram_matrix, STEPS)
        joined = jnp.concatenate([upper_block, lower_block], 1)
        turned = jnp.dot(
            joined, rotation, precision=lax.Precision.HIGHEST, preferred_element_type=jnp.float32
        )
        basis_joined = jnp.concatenate([upper_basis, lower_basis], 1)
        basis_turned = jnp.dot(
            basis_joined,
            rotation,
            precision=lax.Precision.HIGHEST,
            preferred_element_type=jnp.float32,
        )
        upper_block = turned[:, :block_width]
        lower_block = turned[:, block_width:]
        upper_basis = basis_turned[:, :block_width]
        lower_basis = basis_turned[:, block_width:]
        if round_index + 1 < total_rounds:
            send_block = jnp.where(at_start, lower_block, upper_block)
            send_basis = jnp.where(at_start, lower_basis, upper_basis)
            arrived_right = shifted((send_block, send_basis), "col", 1)
            arrived_left = shifted((lower_block, lower_basis), "col", -1)
            new_upper = jnp.where(at_start, upper_block, arrived_right[0])
            new_upper_basis = jnp.where(at_start, upper_basis, arrived_right[1])
            lower_block = jnp.where(at_end, upper_block, arrived_left[0])
            lower_basis = jnp.where(at_end, upper_basis, arrived_left[1])
            upper_block = new_upper
            upper_basis = new_upper_basis
    rotated = jnp.concatenate([upper_block, lower_block], 1)
    basis = jnp.concatenate([upper_basis, lower_basis], 1)
    return (rotated, basis)


def solution(mesh):
    placed = (P("row", "col"), P())
    return jax.shard_map(
        on_device,
        mesh=mesh,
        in_specs=placed,
        out_specs=(P("row", "col"), P("row", "col")),
        check_vma=False,
    )
```

profile of v0, /device:TPU:1, one launch (start us, length us, event | category | flops | bytes accessed | tf_op | source)
XLA Modules:
  0.0 728.8 jit_solution(7407268314713527167)
XLA Ops:
  13.1 7.5 %fusion.13 = f32[256,256]{1,0:T(8,128)} fusion(f32[4096,128]{1,0:T(8,128)S(1)} %get-tuple-element.97, f32[4096,128]{1,0:T(8,128)S(1)} %get-tuple-element.96), kind=kOutput, calls=%fused_computation.41 | convolution fusion | flops 3222274048 | bytes 4456448 | tf_op jit(solution)/shard_map/dot_general | solution.py:69
  20.9 86.2 %all-reduce.3.cloned.1.call-done = f32[256,256]{1,0:T(8,128)} async-done(((f32[256,256]{1,0:T(8,128)}), f32[256,256]{1,0:T(8,128)}) %all-reduce.3.cloned.1.call-update) | async-done | bytes 262160 | tf_op jit(solution)/shard_map/psum | solution.py:76
  107.2 235.1 %while.24 = (s32[]{:T(128)}, f32[256,256]{1,0:T(8,128)}, f32[256,256]{0,1:T(8,128)S(1)}, s32[]{:T(128)}) while((s32[]{:T(128)}, f32[256,256]{1,0:T(8,128)}, f32[256,256]{0,1:T(8,128)S(1)}, s32[]{:T(128)}) %tuple.92), condition=%wide.region_2.3_spmd, body=%wide.region_1.2_spmd.sunk | while | flops 592514 | bytes 6170705 | solution.py:57
  342.3 5.5 fusion.12
  351.1 5.0 collective-permute-start.1
  365.4 13.9 %collective-permute-done.1 = f32[4096,128]{0,1:T(8,128)S(1)} collective-permute-done((f32[4096,128]{0,1:T(8,128)}, f32[4096,128]{0,1:T(8,128)S(1)}, u32[]{:S(2)}, u32[]{:S(2)}) %collective-permute-start.1) | collective-permute-done | bytes 2097184 | tf_op jit(solution)/shard_map/ppermute | solution.py:12
  379.3 4.4 collective-permute-done
  389.0 4.2 fusion.11
  393.8 81.1 %all-reduce.5.cloned.1.call-done = f32[256,256]{1,0:T(8,128)} async-done(((f32[256,256]{1,0:T(8,128)}), f32[256,256]{1,0:T(8,128)}) %all-reduce.5.cloned.1.call-update) | async-done | bytes 262160 | tf_op jit(solution)/shard_map/psum | solution.py:76
  474.9 235.7 %while.25 = (s32[]{:T(128)}, f32[256,256]{1,0:T(8,128)}, f32[256,256]{0,1:T(8,128)S(1)}, s32[]{:T(128)}) while((s32[]{:T(128)}, f32[256,256]{1,0:T(8,128)}, f32[256,256]{0,1:T(8,128)S(1)}, s32[]{:T(128)}) %tuple.95), condition=%wide.region_5.6_spmd, body=%wide.region_4.5_spmd.sunk | while | flops 592514 | bytes 6170705 | solution.py:57
  480.8 4.0 concatenate.83
  490.6 4.0 concatenate.83
  500.4 4.0 concatenate.83
  510.2 4.0 concatenate.83
  520.0 4.0 concatenate.83
  529.9 4.0 concatenate.83
  539.7 4.0 concatenate.83
  549.5 4.0 concatenate.83
  569.1 4.0 concatenate.83
  579.0 4.0 concatenate.83
  588.8 4.0 concatenate.83
  598.6 4.0 concatenate.83
  608.4 4.0 concatenate.83
  618.2 4.0 concatenate.83
  628.1 4.0 concatenate.83
  647.7 4.0 concatenate.83
  657.5 4.0 concatenate.83
  677.2 4.0 concatenate.83
  687.0 4.0 concatenate.83
  696.8 4.0 concatenate.83
  706.6 4.0 concatenate.83
  710.6 10.3 %fusion.10 = f32[4096,256]{1,0:T(8,128)} fusion(f32[256,256]{0,1:T(8,128)S(1)} %get-tuple-element.37, f32[4096,128]{0,1:T(8,128)} %copy-done.3, f32[4096,128]{0,1:T(8,128)S(1)} %get-tuple-element.92), kind=kOutput, calls=%fused_computation.38 | convolution fusion | flops 3222274048 | bytes 8650752 | tf_op jit(solution)/shard_map/dot_general | solution.py:104
  (1164 shorter events, 405.8 us)
Async XLA Ops:
  7.2 100.0 %all-reduce.3.cloned.1.call-start = ((), (), s32[]{:S(2)}) async-start(), calls=%async_computation | async-start | bytes 524288 | tf_op jit(solution)/shard_map/psum | solution.py:76
  20.7 454.2 %all-reduce.5.cloned.1.call-start = ((), (), s32[]{:S(2)}) async-start(), calls=%async_computation.1 | async-start | bytes 524288 | tf_op jit(solution)/shard_map/psum | solution.py:76
  117.0 4.8 copy-start.2
  126.8 4.8 copy-start.2
  136.6 4.8 copy-start.2
  146.4 4.8 copy-start.2
  156.2 4.8 copy-start.2
  166.0 4.8 copy-start.2
  175.8 4.8 copy-start.2
  185.5 4.8 copy-start.2
  195.3 4.8 copy-start.2
  205.1 4.8 copy-start.2
  214.9 4.8 copy-start.2
  224.7 4.8 copy-start.2
  234.5 4.8 copy-start.2
  244.3 4.8 copy-start.2
  254.1 4.8 copy-start.2
  263.9 4.8 copy-start.2
  273.7 4.8 copy-start.2
  293.3 4.8 copy-start.2
  332.5 4.8 copy-start.2
  351.1 28.2 %collective-permute-start.1 = (f32[4096,128]{0,1:T(8,128)}, f32[4096,128]{0,1:T(8,128)S(1)}, u32[]{:S(2)}, u32[]{:S(2)}) collective-permute-start(f32[4096,128]{0,1:T(8,128)} %get-tuple-element.94), channel_id=1, source_target_pairs={{0,16},{16,32},{32,48},{48,64},{64,80},{80,96},{96,112},{1,17},{17... | collective-permute-start | bytes 6291464 | tf_op jit(solution)/shard_map/ppermute | solution.py:12
  356.1 27.7 %collective-permute-start = (f32[4096,128]{0,1:T(8,128)}, f32[4096,128]{0,1:T(8,128)}, u32[]{:S(2)}, u32[]{:S(2)}) collective-permute-start(f32[4096,128]{0,1:T(8,128)} %get-tuple-element.95), channel_id=1, source_target_pairs={{16,0},{32,16},{48,32},{64,48},{80,64},{96,80},{112,96},{17,1},{33... | collective-permute-start | bytes 6291464 | tf_op jit(solution)/shard_map/ppermute | solution.py:12
  359.8 33.4 %collective-permute-start.3 = (f32[128,128]{1,0:T(8,128)S(1)}, f32[128,128]{1,0:T(8,128)S(1)}, u32[]{:S(2)}, u32[]{:S(2)}) collective-permute-start(f32[128,128]{1,0:T(8,128)S(1)} %get-tuple-element.100), channel_id=1, source_target_pairs={{0,16},{16,32},{32,48},{48,64},{64,80},{80,96},{96,112},{1,17},{17... | collective-permute-start | bytes 196616 | tf_op jit(solution)/shard_map/ppermute | solution.py:12
  363.5 29.8 %collective-permute-start.2 = (f32[128,128]{1,0:T(8,128)S(1)}, f32[128,128]{1,0:T(8,128)S(1)}, u32[]{:S(2)}, u32[]{:S(2)}) collective-permute-start(f32[128,128]{1,0:T(8,128)S(1)} %get-tuple-element.101), channel_id=1, source_target_pairs={{16,0},{32,16},{48,32},{64,48},{80,64},{96,80},{112,96},{17,1},{33... | collective-permute-start | bytes 196616 | tf_op jit(solution)/shard_map/ppermute | solution.py:12
  494.5 4.8 copy-start.1
  524.0 4.8 copy-start.1
  543.7 4.8 copy-start.1
  573.1 4.8 copy-start.1
  602.6 4.8 copy-start.1
  651.7 4.8 copy-start.1
  681.1 4.8 copy-start.1
  (26 other events, 115.3 us)
Sparse Core Ops, SparseCore 0:
  20.8 86.3 all-reduce.2
  393.3 81.5 all-reduce.4
where the time goes:
time: 737 us; the launch traced here: 729 us
  local copies, waits for them, and re-layouts  459 us (62%)
  waiting for transfers between devices  186 us (25%)
  matrix products  29 us (4%)
  other arithmetic  21.4 us (3%)
  between operations  14.2 us (2%)
  starting transfers between devices  12.7 us (2%)
    concatenate x144, local copies, waits for them, and re-layouts, turn_columns(): jnp.concatenate([first_part[:, :1], second_part[:, :1], first_part[:, 1:h...  212 us
    psum x2, waiting for transfers between devices, whole_gram(): return lax.psum(local_gram, 'row')  167 us
    gather x48, local copies, waits for them, and re-layouts, rotation_step(): second_diag = jnp.diagonal(current[half_width:, half_width:])  59.8 us
    gather x48, local copies, waits for them, and re-layouts, rotation_step(): coupling = jnp.diagonal(current[:half_width, half_width:])  59.8 us
    gather x48, local copies, waits for them, and re-layouts, rotation_step(): first_diag = jnp.diagonal(current[:half_width, :half_width])  59.8 us
    slice x48, local copies, waits for them, and re-layouts, rotation_step(): first_diag = jnp.diagonal(current[:half_width, :half_width])  46.1 us
    ppermute x4, waiting for transfers between devices, shifted(): return lax.ppermute(value, axis, pairs)  18.3 us
    dot_general x2, matrix products, on_device(): jnp.dot(joined, rotation, precision=lax.Precision.HIGHEST, preferred_elem...  15.8 us
  transfers between devices with their start and end apart: 6, of which 4 were waited for; matrix products, arithmetic and copies ran while one was open for 1% of the time, Pallas kernels for 0%

commit v1 on v0

v1 whole, which is shorter than its diff:
```python
import functools

import jax
import jax.numpy as jnp
from jax import lax
from jax.experimental import pallas as pl
from jax.experimental.pallas import tpu as pltpu
from jax.sharding import PartitionSpec as P

STEPS = 24
H = 128
F32 = jnp.float32
BF16 = jnp.bfloat16
MESH = pl.DeviceIdType.MESH
RAW = 1280
CHUNK = 256


def sublane_total(x):
    x = x + pltpu.roll(x, 4, 0)
    x = x + pltpu.roll(x, 2, 0)
    return x + pltpu.roll(x, 1, 0)


def diagonal(block):
    lane = lax.broadcasted_iota(jnp.int32, (8, H), 1)
    sub = lax.broadcasted_iota(jnp.int32, (8, H), 0)
    acc = jnp.zeros((8, H), F32)
    for i in range(H // 8):
        acc = jnp.where((lane >> 3) == i, block[8 * i : 8 * i + 8, :], acc)
    return sublane_total(jnp.where((lane & 7) == sub, acc, 0.0))


def angles(a, b, d):
    e = b - a
    sign = jnp.where(e >= 0.0, 2.0, -2.0)
    t = sign * d / (jnp.abs(e) + jnp.sqrt(e * e + 4.0 * d * d))
    c = 1.0 / jnp.sqrt(1.0 + t * t)
    return c, t * c


def jacobi(gram, turn):
    lane = lax.broadcasted_iota(jnp.int32, (H, H), 1)
    row = lax.broadcasted_iota(jnp.int32, (H, H), 0)
    eye = (lane == row).astype(F32)
    turn[0] = eye
    turn[1] = jnp.zeros((H, H), F32)
    turn[2] = jnp.zeros((H, H), F32)
    turn[3] = eye

    def rows(top, bottom, c, s):
        f = top * c - bottom * s
        g = top * s + bottom * c
        x = jnp.where(row == 0, g, f)
        u = jnp.where(row == 0, f, pltpu.roll(x, 1, 0))
        v = jnp.where(row == H - 1, f, pltpu.roll(g, H - 1, 0))
        return u, v

    def columns(left, right, c, s):
        f = left * c - right * s
        g = left * s + right * c
        x = jnp.where(lane == 0, g, f)
        u = jnp.where(lane == 0, f, pltpu.roll(x, 1, 1))
        v = jnp.where(lane == H - 1, f, pltpu.roll(g, H - 1, 1))
        return u, v

    def step(_, carry):
        c, s = angles(diagonal(gram[0]), diagonal(gram[3]), diagonal(gram[1]))
        c = jnp.broadcast_to(c[:1], (H, H))
        s = jnp.broadcast_to(s[:1], (H, H))
        ct = jnp.transpose(c)
        st = jnp.transpose(s)
        ut, vt = columns(gram[0], gram[1], c, s)
        ub, vb = columns(gram[2], gram[3], c, s)
        gram[0], gram[2] = rows(ut, ub, ct, st)
        gram[1], gram[3] = rows(vt, vb, ct, st)
        turn[0], turn[2] = rows(turn[0], turn[2], ct, st)
        turn[1], turn[3] = rows(turn[1], turn[3], ct, st)
        return carry

    lax.fori_loop(0, STEPS, step, 0)


def load_gram(gram, a, c, d, flipped):
    ct = jnp.transpose(c)
    gram[0] = jnp.where(flipped, d, a)
    gram[1] = jnp.where(flipped, ct, c)
    gram[2] = jnp.where(flipped, c, ct)
    gram[3] = jnp.where(flipped, a, d)


def rotation(turn, flipped):
    t0, t1, t2, t3 = turn[0], turn[1], turn[2], turn[3]
    up = jnp.concatenate([jnp.where(flipped, t1, t0), jnp.where(flipped, t0, t1)], 1)
    lo = jnp.concatenate([jnp.where(flipped, t3, t2), jnp.where(flipped, t2, t3)], 1)
    return jnp.transpose(up), jnp.transpose(lo)


def split(x):
    hi = x.astype(BF16)
    lo = (x - hi.astype(F32)).astype(BF16)
    return hi, lo


def dot(x, y):
    return lax.dot_general(x, y, (((1,), (0,)), ((), ())), preferred_element_type=F32)


def dot_t(x, y):
    return lax.dot_general(x, y, (((0,), (0,)), ((), ())), preferred_element_type=F32)


def product(x, w_hi, w_lo):
    hi, lo = split(x)
    return dot(hi, w_hi) + (dot(hi, w_lo) + dot(lo, w_hi))


def first_kernel(
    n_col, n_row,
    x_ref, ori_ref,
    u_out, l_out, pack_l_out, pack_r_out, c_out,
    b, raw_l, raw_r, u2, l2, send_r, send_x, acc, part, rs_buf, total, gram, turn,
    pack_send, pack_l, pack_r, w_hi, w_lo, acc2, part2, rs2_buf, total2,
    load_sem, rs_send, rs_recv, ag_send, ag_recv, rs2_send, rs2_recv, ag2_send, ag2_recv,
    raw_send, raw_recv, pack_ssem, pack_rsem, r_send, r_recv, x_send, x_recv, out_sem,
):
    rows = b.shape[0]
    col = lax.axis_index("col")
    row = lax.axis_index("row")
    first = col == 0
    last = col == n_col - 1
    right = lax.rem(col + 1, n_col)
    left = lax.rem(col + n_col - 1, n_col)

    barrier = pltpu.get_barrier_semaphore()
    for o in range(1, n_row):
        pl.semaphore_signal(
            barrier, inc=1, device_id={"row": lax.rem(row + o, n_row)}, device_id_type=MESH
        )
    for side in (left, right):
        pl.semaphore_signal(barrier, inc=1, device_id={"col": side}, device_id_type=MESH)

    n_load = load_sem.shape[0]
    step = rows // n_load

    def load(i):
        part_rows = pl.ds(pl.multiple_of(i * step, 8), step)
        return pltpu.make_async_copy(x_ref.at[part_rows], b.at[part_rows], load_sem.at[i])

    for i in range(n_load):
        load(i).start()

    def right_start(src, dst, ssem, rsem):
        @pl.when(jnp.logical_not(last))
        def _():
            pltpu.make_async_remote_copy(
                src, dst[0], ssem, rsem.at[0], device_id={"col": right}, device_id_type=MESH
            ).start()

        @pl.when(last)
        def _():
            pltpu.make_async_copy(src, dst[1], rsem.at[1]).start()

    def left_start(src, dst, ssem, rsem):
        @pl.when(jnp.logical_not(first))
        def _():
            pltpu.make_async_remote_copy(
                src, dst[1], ssem, rsem.at[1], device_id={"col": left}, device_id_type=MESH
            ).start()

        @pl.when(first)
        def _():
            pltpu.make_async_copy(src, dst[0], rsem.at[0]).start()

    def arrived(dst, sem):
        pltpu.make_async_copy(dst, dst, sem).wait()

    def right_sent(src, ssem):
        @pl.when(jnp.logical_not(last))
        def _():
            pltpu.make_async_copy(src, src, ssem).wait()

    def left_sent(src, ssem):
        @pl.when(jnp.logical_not(first))
        def _():
            pltpu.make_async_copy(src, src, ssem).wait()

    acc[...] = jnp.zeros_like(acc)

    def gram_part(i):
        load(i).wait()
        hi, lo = split(b[pl.ds(pl.multiple_of(i * step, 8), step), :])
        acc[...] += dot_t(hi, jnp.concatenate([hi, lo], 1))

    n_first = -(-RAW // step)
    lax.fori_loop(0, n_first, lambda i, c: (gram_part(i), c)[1], 0)
    pl.semaphore_wait(barrier, n_row + 1)
    raw_src = b.at[pl.ds(0, RAW)]
    right_start(raw_src, (raw_l, raw_r), raw_send.at[0], raw_recv)
    left_start(raw_src, (raw_l, raw_r), raw_send.at[1], raw_recv)
    lax.fori_loop(n_first, n_load, lambda i, c: (gram_part(i), c)[1], 0)
    cross = acc[:H, 3 * H :] + jnp.transpose(acc[H:, 2 * H : 3 * H])
    part[:H] = acc[:H, :H] + (acc[:H, 2 * H : 3 * H] + jnp.transpose(acc[:H, 2 * H : 3 * H]))
    part[H : 2 * H] = acc[:H, H : 2 * H] + cross
    part[2 * H :] = acc[H:, H : 2 * H] + (acc[H:, 3 * H :] + jnp.transpose(acc[H:, 3 * H :]))

    def all_reduce(local, buf, whole, s_send, s_recv, g_send, g_recv):
        size = buf.shape[1]
        mine = pl.ds(pl.multiple_of(row * size, 8), size)

        def scatter(o):
            peer = lax.rem(row + o, n_row)
            return pltpu.make_async_remote_copy(
                local.at[pl.ds(pl.multiple_of(peer * size, 8), size)], buf.at[o],
                s_send.at[o], s_recv.at[o], device_id={"row": peer}, device_id_type=MESH,
            )

        def gather(o):
            peer = lax.rem(row + o, n_row)
            return pltpu.make_async_remote_copy(
                whole.at[mine], whole.at[mine],
                g_send.at[o], g_recv.at[o], device_id={"row": peer}, device_id_type=MESH,
            )

        for o in range(1, n_row):
            scatter(o).start()
        value = local[mine, :]
        for o in range(1, n_row):
            scatter(o).wait_recv()
            value = value + buf[o]
        whole[mine, :] = value
        for o in range(1, n_row):
            gather(o).start()
        for o in range(1, n_row):
            gather(o).wait_recv()
        for o in range(1, n_row):
            scatter(o).wait_send()
            gather(o).wait_send()

    all_reduce(part, rs_buf, total, rs_send, rs_recv, ag_send, ag_recv)

    flipped = ori_ref[0, col] == 1
    load_gram(gram, total[:H], total[H : 2 * H], total[2 * H :], flipped)
    jacobi(gram, turn)
    up, lo = rotation(turn, flipped)
    w_r = jnp.where(first, lo, up)
    w_x = jnp.where(first, up, lo)
    pack_send[0, : 2 * H] = w_r
    pack_send[0, 2 * H :] = jnp.where(first, gram[3], gram[0])
    pack_send[1, : 2 * H] = w_x
    pack_send[1, 2 * H :] = jnp.where(first, gram[0], gram[3])
    right_start(pack_send.at[0], (pack_l, pack_r), pack_ssem.at[0], pack_rsem)
    left_start(pack_send.at[1], (pack_l, pack_r), pack_ssem.at[1], pack_rsem)
    hi, lo = split(jnp.concatenate([w_r, w_x], 1))
    w_hi[...] = hi
    w_lo[...] = lo

    n_turn = (rows - RAW) // CHUNK

    def late(i):
        return pl.ds(pl.multiple_of(RAW + i * CHUNK, 8), CHUNK)

    def sent(i):
        return pl.ds(pl.multiple_of(i * CHUNK, 8), CHUNK)

    def turn_part(i, carry):
        turned = product(b[late(i), :], w_hi[...], w_lo[...])
        send_r[sent(i), :] = turned[:, :H]
        send_x[sent(i), :] = turned[:, H:]
        dst = (u2.at[late(i)], l2.at[late(i)])
        right_start(send_r.at[sent(i)], dst, r_send.at[i], r_recv.at[i])
        left_start(send_x.at[sent(i)], dst, x_send.at[i], r_recv.at[i])
        return carry

    lax.fori_loop(0, n_turn, turn_part, 0)

    acc2[...] = jnp.zeros_like(acc2)

    def cross_part(at):
        u_hi, u_lo = split(u2[at, :])
        l_hi, l_lo = split(l2[at, :])
        acc2[...] += dot_t(
            jnp.concatenate([u_hi, u_lo], 1), jnp.concatenate([l_hi, l_lo], 1)
        )
        slot = at.start // CHUNK
        pltpu.make_async_copy(u2.at[at], u_out.at[at], out_sem.at[0, slot]).start()
        pltpu.make_async_copy(l2.at[at], l_out.at[at], out_sem.at[1, slot]).start()

    arrived(raw_l, raw_recv.at[0])
    arrived(raw_r, raw_recv.at[1])
    arrived(pack_l, pack_rsem.at[0])
    arrived(pack_r, pack_rsem.at[1])
    out_l = pltpu.make_async_copy(pack_l, pack_l_out, out_sem.at[0, rows // CHUNK])
    out_r = pltpu.make_async_copy(pack_r, pack_r_out, out_sem.at[1, rows // CHUNK])
    out_l.start()
    out_r.start()
    wl_hi, wl_lo = split(pack_l[: 2 * H])
    wr_hi, wr_lo = split(pack_r[: 2 * H])
    w_hi[...] = jnp.concatenate([wl_hi, wr_hi], 1)
    w_lo[...] = jnp.concatenate([wl_lo, wr_lo], 1)

    def raw_part(i, carry):
        at = pl.ds(pl.multiple_of(i * CHUNK, 8), CHUNK)
        u2[at, :] = product(raw_l[at, :], w_hi[:, :H], w_lo[:, :H])
        l2[at, :] = product(raw_r[at, :], w_hi[:, H:], w_lo[:, H:])
        cross_part(at)
        return carry

    lax.fori_loop(0, RAW // CHUNK, raw_part, 0)

    def late_part(i, carry):
        arrived(u2.at[late(i)], r_recv.at[i, 0])
        arrived(l2.at[late(i)], r_recv.at[i, 1])
        cross_part(late(i))
        return carry

    lax.fori_loop(0, n_turn, late_part, 0)
    part2[...] = (acc2[:H, :H] + acc2[H:, H:]) + (acc2[:H, H:] + acc2[H:, :H])
    all_reduce(part2, rs2_buf, total2, rs2_send, rs2_recv, ag2_send, ag2_recv)
    out_c = pltpu.make_async_copy(total2, c_out, load_sem.at[0])
    out_c.start()

    right_sent(raw_src, raw_send.at[0])
    left_sent(raw_src, raw_send.at[1])
    right_sent(pack_send.at[0], pack_ssem.at[0])
    left_sent(pack_send.at[1], pack_ssem.at[1])

    def drain(i, carry):
        right_sent(send_r.at[sent(i)], r_send.at[i])
        left_sent(send_x.at[sent(i)], x_send.at[i])
        return carry

    lax.fori_loop(0, n_turn, drain, 0)

    def written(i, carry):
        at = pl.ds(pl.multiple_of(i * CHUNK, 8), CHUNK)
        pltpu.make_async_copy(u2.at[at], u_out.at[at], out_sem.at[0, i]).wait()
        pltpu.make_async_copy(l2.at[at], l_out.at[at], out_sem.at[1, i]).wait()
        return carry

    lax.fori_loop(0, rows // CHUNK, written, 0)
    out_l.wait()
    out_r.wait()
    out_c.wait()


def first_round(n_col, n_row, snapshots, orientation):
    rows = snapshots.shape[0]
    late = rows - RAW
    n_turn = late // CHUNK
    sem = pltpu.SemaphoreType.DMA
    any_spec = pl.BlockSpec(memory_space=pl.ANY)
    return pl.pallas_call(
        functools.partial(first_kernel, n_col, n_row),
        out_shape=[
            jax.ShapeDtypeStruct((rows, H), F32),
            jax.ShapeDtypeStruct((rows, H), F32),
            jax.ShapeDtypeStruct((3 * H, H), F32),
            jax.ShapeDtypeStruct((3 * H, H), F32),
            jax.ShapeDtypeStruct((H, H), F32),
        ],
        in_specs=[any_spec, pl.BlockSpec(memory_space=pltpu.SMEM)],
        out_specs=[any_spec] * 5,
        scratch_shapes=[
            pltpu.VMEM((rows, 2 * H), F32),
            pltpu.VMEM((RAW, 2 * H), F32),
            pltpu.VMEM((RAW, 2 * H), F32),
            pltpu.VMEM((rows, H), F32),
            pltpu.VMEM((rows, H), F32),
            pltpu.VMEM((late, H), F32),
            pltpu.VMEM((late, H), F32),
            pltpu.VMEM((2 * H, 4 * H), F32),
            pltpu.VMEM((3 * H, H), F32),
            pltpu.VMEM((n_row, 3 * H // n_row, H), F32),
            pltpu.VMEM((3 * H, H), F32),
            pltpu.VMEM((4, H, H), F32),
            pltpu.VMEM((4, H, H), F32),
            pltpu.VMEM((2, 3 * H, H), F32),
            pltpu.VMEM((3 * H, H), F32),
            pltpu.VMEM((3 * H, H), F32),
            pltpu.VMEM((2 * H, 2 * H), BF16),
            pltpu.VMEM((2 * H, 2 * H), BF16),
            pltpu.VMEM((2 * H, 2 * H), F32),
            pltpu.VMEM((H, H), F32),
            pltpu.VMEM((n_row, H // n_row, H), F32),
            pltpu.VMEM((H, H), F32),
            sem((8,)),
            sem((n_row,)), sem((n_row,)), sem((n_row,)), sem((n_row,)),
            sem((n_row,)), sem((n_row,)), sem((n_row,)), sem((n_row,)),
            sem((2,)), sem((2,)), sem((2,)), sem((2,)),
            sem((n_turn,)), sem((n_turn, 2)), sem((n_turn,)), sem((1,)),
            sem((2, rows // CHUNK + 1)),
        ],
        compiler_params=pltpu.CompilerParams(
            collective_id=0, has_side_effects=True, vmem_limit_bytes=48 * 2**20
        ),
    )(snapshots, orientation)


def last_kernel(
    n_col,
    u_ref, l_ref, pack_l, pack_r, c_ref, ori_ref,
    out_ref, basis_ref,
    u, l, out, basis, gram, turn, w_hi, w_lo, load_sem, out_sem,
):
    rows = u.shape[0]
    col = lax.axis_index("col")
    row = lax.axis_index("row")
    load_u = pltpu.make_async_copy(u_ref, u, load_sem.at[0])
    load_l = pltpu.make_async_copy(l_ref, l, load_sem.at[1])
    load_u.start()
    load_l.start()
    flipped = ori_ref[1, col] == 1
    load_gram(gram, pack_l[2 * H :], c_ref[...], pack_r[2 * H :], flipped)
    jacobi(gram, turn)
    up, lo = rotation(turn, flipped)
    hi, lo = split(jnp.concatenate([up, lo], 1))
    w_hi[...] = hi
    w_lo[...] = lo

    def finish(at):
        return pltpu.make_async_copy(out.at[at], out_ref.at[at], out_sem.at[at.start // CHUNK])

    load_u.wait()
    load_l.wait()

    def turn_part(i, carry):
        at = pl.ds(pl.multiple_of(i * CHUNK, 8), CHUNK)
        joined = jnp.concatenate([u[at, :], l[at, :]], 1)
        out[at, :] = product(joined, w_hi[...], w_lo[...])
        finish(at).start()
        return carry

    lax.fori_loop(0, rows // CHUNK, turn_part, 0)

    group = row // 2
    lower_half = row % 2 == 1
    from_left = jnp.maximum(col - 1, 0)
    from_right = jnp.minimum(col + 1, n_col - 1)
    basis_l = jnp.where(lower_half, pack_l[H : 2 * H], pack_l[:H])
    basis_r = jnp.where(lower_half, pack_r[H : 2 * H], pack_r[:H])
    basis_l = jnp.where(group == from_left, basis_l, 0.0)
    basis_r = jnp.where(group == from_right, basis_r, 0.0)
    basis[...] = product(jnp.concatenate([basis_l, basis_r], 1), w_hi[...], w_lo[...])
    out_basis = pltpu.make_async_copy(basis, basis_ref, load_sem.at[0])
    out_basis.start()

    def written(i, carry):
        finish(pl.ds(pl.multiple_of(i * CHUNK, 8), CHUNK)).wait()
        return carry

    lax.fori_loop(0, rows // CHUNK, written, 0)
    out_basis.wait()


def last_round(n_col, n_row, u2, l2, pack_l, pack_r, cross, orientation):
    rows = u2.shape[0]
    basis_rows = 2 * H * n_col // n_row
    sem = pltpu.SemaphoreType.DMA
    any_spec = pl.BlockSpec(memory_space=pl.ANY)
    vmem = pl.BlockSpec(memory_space=pltpu.VMEM)
    return pl.pallas_call(
        functools.partial(last_kernel, n_col),
        out_shape=[
            jax.ShapeDtypeStruct((rows, 2 * H), F32),
            jax.ShapeDtypeStruct((basis_rows, 2 * H), F32),
        ],
        in_specs=[any_spec, any_spec, vmem, vmem, vmem, pl.BlockSpec(memory_space=pltpu.SMEM)],
        out_specs=[any_spec] * 2,
        scratch_shapes=[
            pltpu.VMEM((rows, H), F32),
            pltpu.VMEM((rows, H), F32),
            pltpu.VMEM((rows, 2 * H), F32),
            pltpu.VMEM((basis_rows, 2 * H), F32),
            pltpu.VMEM((4, H, H), F32),
            pltpu.VMEM((4, H, H), F32),
            pltpu.VMEM((2 * H, 2 * H), BF16),
            pltpu.VMEM((2 * H, 2 * H), BF16),
            sem((2,)),
            sem((rows // CHUNK,)),
        ],
        compiler_params=pltpu.CompilerParams(vmem_limit_bytes=32 * 2**20),
    )(u2, l2, pack_l, pack_r, cross, orientation)


def on_device(n_col, n_row, snapshots, orientation):
    moved = first_round(n_col, n_row, snapshots, orientation)
    return tuple(last_round(n_col, n_row, *moved, orientation))


def solution(mesh):
    return jax.shard_map(
        functools.partial(on_device, mesh.shape["col"], mesh.shape["row"]),
        mesh=mesh,
        in_specs=(P("row", "col"), P()),
        out_specs=(P("row", "col"), P("row", "col")),
        check_vma=False,
    )
```

time: 737 us -> 73.4 us (0.10); the launches traced: 729 us -> 73.3 us
  local copies, waits for them, and re-layouts: 459 us -> 0.67 us
  waiting for transfers between devices: 186 us -> 0 us
  Pallas kernels: 0 us -> 72 us
  matrix products: 29 us -> 0 us
  other arithmetic: 21.4 us -> 0 us
  between operations: 14.2 us -> 0.65 us
  starting transfers between devices: 12.7 us -> 0 us
    concatenate x144 -> x0, local copies, waits for them, and re-layouts: 212 us -> none  [turn_columns(): jnp.concatenate([first_part[:, :1], second_part[:, :1], first_part[:, 1:h...]
    gather x144 -> x0, local copies, waits for them, and re-layouts: 179 us -> none  [the longest x48 59.8 us: rotation_step(): second_diag = jnp.diagonal(current[half_width:, half_width:])]
    psum x2 -> x0, waiting for transfers between devices: 167 us -> none  [whole_gram(): return lax.psum(local_gram, 'row')]
    pallas_call x0 -> x2, Pallas kernels: none -> 72 us  [the longest x1 58.8 us: first_round(): pl.pallas_call(functools.partial(first_kernel, n_col, n_row), out_shape=[...]
    slice x529 -> x0, local copies, waits for them, and re-layouts: 63.3 us -> none  [the longest x48 46.1 us: rotation_step(): first_diag = jnp.diagonal(current[:half_width, :half_width])]
    dot_general x6 -> x0, matrix products: 29 us -> none  [the longest x2 15.8 us: on_device(): jnp.dot(joined, rotation, precision=lax.Precision.HIGHEST, preferred_elem...]
    ppermute x4 -> x0, waiting for transfers between devices: 18.3 us -> none  [shifted(): return lax.ppermute(value, axis, pairs)]
    ppermute x4 -> x0, starting transfers between devices: 12.5 us -> none  [shifted(): return lax.ppermute(value, axis, pairs)]
  transfers between devices with their start and end apart: 6 -> 0, of which waited for: 4 -> 0; matrix products, arithmetic and copies ran while one was open for 1% -> 0% of each run, Pallas kernels for 0% -> 0%
where the time goes in v1:
time: 73.4 us; the launch traced here: 73.3 us
  Pallas kernels  72 us (98%)
    pallas_call x1, Pallas kernels, first_round(): pl.pallas_call(functools.partial(first_kernel, n_col, n_row), out_shape=[...  58.8 us
    pallas_call x1, Pallas kernels, last_round(): pl.pallas_call(functools.partial(last_kernel, n_col), out_shape=[jax.Shap...  13.2 us

profile of v1, /device:TPU:1, one launch (start us, length us, event | category | flops | bytes accessed | tf_op | source)
XLA Modules:
  0.0 73.3 jit_solution(16827641731376408080)
XLA Ops:
  0.6 0.0 copy-start
  0.6 0.7 copy-done
  1.3 58.8 %shard_map.41 = (f32[4096,128]{1,0:T(8,128)S(1)}, f32[4096,128]{1,0:T(8,128)S(1)}, f32[384,128]{1,0:T(8,128)S(1)}, f32[384,128]{1,0:T(8,128)S(1)}, f32[128,128]{1,0:T(8,128)S(1)}) custom-call(f32[4096,256]{1,0:T(8,128)} %x_ref.1, s32[2,8]{1,0:T(2,128)S(1)} %copy-done), custom_call_target="tpu_custom_call" | custom-call | tf_op jit(solution)/shard_map/pallas_call | solution.py:353
  60.1 13.2 %shard_map.42 = (f32[4096,256]{1,0:T(8,128)}, f32[128,256]{1,0:T(8,128)}) custom-call(f32[4096,128]{1,0:T(8,128)S(1)} %get-tuple-element.7.u_ref, f32[4096,128]{1,0:T(8,128)S(1)} %get-tuple-element.8.l_ref, f32[384,128]{1,0:T(8,128)S(1)} %get-tuple-element.9.pack_l, f32[384,128]{1,0:T(8,128)S(1)} %get-tuple-element.10.pack_r, ...), custom_call_target="tpu_custom_call" | custom-call | tf_op jit(solution)/shard_map/pallas_call | solution.py:462
Async XLA Ops:
  0.6 0.7 copy-start

commit v2 on v1

v2 whole, which is shorter than its diff:
```python
import functools

import jax
import jax.numpy as jnp
from jax import lax
from jax.experimental import pallas as pl
from jax.experimental.pallas import tpu as pltpu
from jax.sharding import PartitionSpec as P

STEPS = 24
H = 128
F32 = jnp.float32
BF16 = jnp.bfloat16
MESH = pl.DeviceIdType.MESH
RAW = 1280
CHUNK = 256
OUT_CHUNK = 512
PAD = 8
UNROLL = 8
SQRT_HALF = 0.5**0.5


def angles(a, b, d):
    e = b - a
    scale = pltpu.reciprocal(jnp.maximum(jnp.abs(e), jnp.abs(d)), approx=True)
    scale = jnp.where(e >= 0.0, scale, -scale)
    e = e * scale
    dd = (d + d) * scale
    r = lax.rsqrt(e * e + dd * dd)
    cc = e * r + 1.0
    q = lax.rsqrt(cc)
    ss = dd * r
    half = q * SQRT_HALF
    return cc * half, ss * half, (ss * (q * q)) * d


def jacobi(state, a, c, d, flipped):
    lane = lax.broadcasted_iota(jnp.int32, (H, H), 1)
    row = lax.broadcasted_iota(jnp.int32, (H, H), 0)
    eye = (lane == row).astype(F32)
    zero = jnp.zeros((H, H), F32)
    ct = jnp.transpose(c)
    upper = jnp.where(flipped, d, a)
    lower = jnp.where(flipped, a, d)
    held = slice(PAD, PAD + H)
    state[0, 0, held] = upper
    state[0, 1, held] = jnp.where(flipped, ct, c)
    state[0, 2, held] = eye
    state[0, 3, held] = zero
    state[0, 4, held] = jnp.broadcast_to(jnp.sum(upper * eye, axis=1, keepdims=True), (H, H))
    state[0, 5, held] = jnp.where(flipped, c, ct)
    state[0, 6, held] = lower
    state[0, 7, held] = zero
    state[0, 8, held] = eye
    state[0, 9, held] = jnp.broadcast_to(jnp.sum(lower * eye, axis=1, keepdims=True), (H, H))

    def put(dst, k, i, f, g):
        r = PAD + 8 * i
        if i == 0:
            state[dst, k, r : r + 1] = f[:1]
            state[dst, k, r + 1 : r + 2] = g[:1]
            state[dst, k, r + 2 : r + 9] = f[1:]
            state[dst, k + 5, r : r + 7] = g[1:]
        elif i == H // 8 - 1:
            state[dst, k, r + 1 : r + 8] = f[:7]
            state[dst, k + 5, r - 1 : r + 7] = g
            state[dst, k + 5, r + 7 : r + 8] = f[7:]
        else:
            state[dst, k, r + 1 : r + 9] = f
            state[dst, k + 5, r - 1 : r + 7] = g

    def step(src, dst):
        for i in range(H // 8):
            r = slice(PAD + 8 * i, PAD + 8 * i + 8)
            u = [state[src, k, r] for k in range(5)]
            l = [state[src, k + 5, r] for k in range(5)]
            dot_ul = jnp.sum(u[2] * l[0] + u[3] * l[1], axis=1, keepdims=True)
            dot_ul = jnp.broadcast_to(dot_ul, (8, H))
            cos, sin, shift = angles(u[4], l[4], dot_ul)
            for k in range(4):
                put(dst, k, i, u[k] * cos - l[k] * sin, u[k] * sin + l[k] * cos)
            put(dst, 4, i, u[4] - shift, l[4] + shift)

    def several(_, carry):
        for _ in range(UNROLL // 2):
            step(0, 1)
            step(1, 0)
        return carry

    lax.fori_loop(0, STEPS // UNROLL, several, 0)


def final_gram(state, k):
    held = slice(PAD, PAD + H)
    y = jnp.concatenate([state[0, k, held], state[0, k + 1, held]], 1)
    w = jnp.concatenate([state[0, k + 2, held], state[0, k + 3, held]], 1)
    return lax.dot_general(
        w, y, (((1,), (1,)), ((), ())),
        precision=lax.Precision.HIGHEST, preferred_element_type=F32,
    )


def rotation(state, flipped):
    held = slice(PAD, PAD + H)
    halves = []
    for k in (2, 7):
        left, right = state[0, k, held], state[0, k + 1, held]
        halves.append(
            jnp.transpose(
                jnp.concatenate(
                    [jnp.where(flipped, right, left), jnp.where(flipped, left, right)], 1
                )
            )
        )
    return halves


def split(x):
    hi = x.astype(BF16)
    lo = (x - hi.astype(F32)).astype(BF16)
    return hi, lo


def dot(x, y):
    return lax.dot_general(x, y, (((1,), (0,)), ((), ())), preferred_element_type=F32)


def dot_t(x, y):
    return lax.dot_general(x, y, (((0,), (0,)), ((), ())), preferred_element_type=F32)


def sum_of(terms):
    while len(terms) > 1:
        terms = [sum(terms[i : i + 2][1:], terms[i]) for i in range(0, len(terms), 2)]
    return terms[0]


def product(x, w_hi, w_lo):
    hi, lo = split(x)
    return dot(hi, w_hi) + (dot(hi, w_lo) + dot(lo, w_hi))


def first_kernel(
    n_col, n_row,
    x_ref, ori_ref,
    u_out, l_out, pack_out, c_out,
    b, raw_l, raw_r, u2, l2, send_r, send_x, acc, part, rs_buf, total, state,
    pack_send, pack, w_hi, w_lo, acc2, part2, buf_0, buf_1, total2, ori,
    load_sem, rs_send, rs_recv, ag_send, ag_recv, s2_send, s2_recv, pag_send, pag_recv,
    raw_send, raw_recv, pack_ssem, pack_rsem, r_send, r_recv, x_send, out_sem,
):
    rows = b.shape[0]
    col = lax.axis_index("col")
    row = lax.axis_index("row")
    first = col == 0
    last = col == n_col - 1
    right = lax.rem(col + 1, n_col)
    left = lax.rem(col + n_col - 1, n_col)

    barrier = pltpu.get_barrier_semaphore()
    for o in range(1, n_row):
        pl.semaphore_signal(
            barrier, inc=1, device_id={"row": lax.rem(row + o, n_row)}, device_id_type=MESH
        )
    for side in (left, right):
        pl.semaphore_signal(barrier, inc=1, device_id={"col": side}, device_id_type=MESH)

    n_load = load_sem.shape[0]
    step = rows // n_load

    def load(i):
        part_rows = pl.ds(pl.multiple_of(i * step, 8), step)
        return pltpu.make_async_copy(x_ref.at[part_rows], b.at[part_rows], load_sem.at[i])

    for i in range(n_load):
        load(i).start()
    get_ori = pltpu.make_async_copy(ori_ref, ori, out_sem.at[0, rows // CHUNK])
    get_ori.start()

    def right_start(src, dst, ssem, rsem):
        @pl.when(jnp.logical_not(last))
        def _():
            pltpu.make_async_remote_copy(
                src, dst[0], ssem, rsem.at[0], device_id={"col": right}, device_id_type=MESH
            ).start()

        @pl.when(last)
        def _():
            pltpu.make_async_copy(src, dst[1], rsem.at[1]).start()

    def left_start(src, dst, ssem, rsem):
        @pl.when(jnp.logical_not(first))
        def _():
            pltpu.make_async_remote_copy(
                src, dst[1], ssem, rsem.at[1], device_id={"col": left}, device_id_type=MESH
            ).start()

        @pl.when(first)
        def _():
            pltpu.make_async_copy(src, dst[0], rsem.at[0]).start()

    def arrived(dst, sem):
        pltpu.make_async_copy(dst, dst, sem).wait()

    def right_sent(src, ssem):
        @pl.when(jnp.logical_not(last))
        def _():
            pltpu.make_async_copy(src, src, ssem).wait()

    def left_sent(src, ssem):
        @pl.when(jnp.logical_not(first))
        def _():
            pltpu.make_async_copy(src, src, ssem).wait()

    acc[...] = jnp.zeros_like(acc)

    def gram_part(i):
        load(i).wait()
        hi, lo = split(b[pl.ds(pl.multiple_of(i * step, 8), step), :])
        acc[...] += dot_t(hi, jnp.concatenate([hi, lo], 1))

    n_first = -(-RAW // step)
    lax.fori_loop(0, n_first, lambda i, c: (gram_part(i), c)[1], 0)
    pl.semaphore_wait(barrier, n_row + 1)
    raw_src = b.at[pl.ds(0, RAW)]
    right_start(raw_src, (raw_l, raw_r), raw_send.at[0], raw_recv)
    left_start(raw_src, (raw_l, raw_r), raw_send.at[1], raw_recv)
    lax.fori_loop(n_first, n_load, lambda i, c: (gram_part(i), c)[1], 0)
    cross = acc[:H, 3 * H :] + jnp.transpose(acc[H:, 2 * H : 3 * H])
    part[:H] = acc[:H, :H] + (acc[:H, 2 * H : 3 * H] + jnp.transpose(acc[:H, 2 * H : 3 * H]))
    part[H : 2 * H] = acc[:H, H : 2 * H] + cross
    part[2 * H :] = acc[H:, H : 2 * H] + (acc[H:, 3 * H :] + jnp.transpose(acc[H:, 3 * H :]))

    def all_reduce(local, buf, whole, s_send, s_recv, g_send, g_recv):
        size = buf.shape[1]
        mine = pl.ds(pl.multiple_of(row * size, 8), size)

        def scatter(o):
            peer = lax.rem(row + o, n_row)
            return pltpu.make_async_remote_copy(
                local.at[pl.ds(pl.multiple_of(peer * size, 8), size)], buf.at[o],
                s_send.at[o], s_recv.at[o], device_id={"row": peer}, device_id_type=MESH,
            )

        def gather(o):
            peer = lax.rem(row + o, n_row)
            return pltpu.make_async_remote_copy(
                whole.at[mine], whole.at[mine],
                g_send.at[o], g_recv.at[o], device_id={"row": peer}, device_id_type=MESH,
            )

        for o in range(1, n_row):
            scatter(o).start()
        value = local[mine, :]
        for o in range(1, n_row):
            scatter(o).wait_recv()
            value = value + buf[o]
        whole[mine, :] = value
        for o in range(1, n_row):
            gather(o).start()
        for o in range(1, n_row):
            gather(o).wait_recv()
        for o in range(1, n_row):
            scatter(o).wait_send()
            gather(o).wait_send()

    all_reduce(part, rs_buf, total, rs_send, rs_recv, ag_send, ag_recv)

    get_ori.wait()
    flipped = ori[0, col] == 1
    jacobi(state, total[:H], total[H : 2 * H], total[2 * H :], flipped)
    up, lo = rotation(state, flipped)
    gram_up, gram_lo = final_gram(state, 0), final_gram(state, 5)
    w_r = jnp.where(first, lo, up)
    w_x = jnp.where(first, up, lo)
    pack_send[0, : 2 * H] = w_r
    pack_send[0, 2 * H :] = jnp.where(first, gram_lo, gram_up)
    pack_send[1, : 2 * H] = w_x
    pack_send[1, 2 * H :] = jnp.where(first, gram_up, gram_lo)
    slice_rows = 3 * H // n_row
    mine = pl.ds(pl.multiple_of(row * slice_rows, 8), slice_rows)
    pack_dst = (pack.at[0, mine], pack.at[1, mine])
    right_start(pack_send.at[0, mine], pack_dst, pack_ssem.at[0], pack_rsem)
    left_start(pack_send.at[1, mine], pack_dst, pack_ssem.at[1], pack_rsem)
    hi, lo = split(jnp.concatenate([w_r, w_x], 1))
    w_hi[...] = hi
    w_lo[...] = lo

    n_turn = (rows - RAW) // CHUNK

    def late(i):
        return pl.ds(pl.multiple_of(RAW + i * CHUNK, 8), CHUNK)

    def sent(i):
        return pl.ds(pl.multiple_of(i * CHUNK, 8), CHUNK)

    def turn_part(i, carry):
        turned = product(b[late(i), :], w_hi[...], w_lo[...])
        send_r[sent(i), :] = turned[:, :H]
        send_x[sent(i), :] = turned[:, H:]
        dst = (u2.at[late(i)], l2.at[late(i)])
        right_start(send_r.at[sent(i)], dst, r_send.at[i], r_recv.at[i])
        left_start(send_x.at[sent(i)], dst, x_send.at[i], r_recv.at[i])
        return carry

    lax.fori_loop(0, n_turn, turn_part, 0)

    acc2[...] = jnp.zeros_like(acc2)

    def cross_part(at):
        u_hi, u_lo = split(u2[at, :])
        l_hi, l_lo = split(l2[at, :])
        acc2[...] += dot_t(
            jnp.concatenate([u_hi, u_lo], 1), jnp.concatenate([l_hi, l_lo], 1)
        )
        slot = at.start // CHUNK
        pltpu.make_async_copy(u2.at[at], u_out.at[at], out_sem.at[0, slot]).start()
        pltpu.make_async_copy(l2.at[at], l_out.at[at], out_sem.at[1, slot]).start()

    def pass_on(o):
        return pltpu.make_async_remote_copy(
            pack.at[:, mine], pack.at[:, mine], pag_send.at[o], pag_recv.at[o],
            device_id={"row": lax.rem(row + o, n_row)}, device_id_type=MESH,
        )

    arrived(pack_dst[0], pack_rsem.at[0])
    arrived(pack_dst[1], pack_rsem.at[1])
    for o in range(1, n_row):
        pass_on(o).start()
    arrived(raw_l, raw_recv.at[0])
    arrived(raw_r, raw_recv.at[1])
    for o in range(1, n_row):
        pass_on(o).wait_recv()
    out_pack = pltpu.make_async_copy(pack, pack_out, out_sem.at[1, rows // CHUNK])
    out_pack.start()
    wl_hi, wl_lo = split(pack[0, : 2 * H])
    wr_hi, wr_lo = split(pack[1, : 2 * H])
    w_hi[...] = jnp.concatenate([wl_hi, wr_hi], 1)
    w_lo[...] = jnp.concatenate([wl_lo, wr_lo], 1)

    def raw_part(i, carry):
        at = pl.ds(pl.multiple_of(i * CHUNK, 8), CHUNK)
        u2[at, :] = product(raw_l[at, :], w_hi[:, :H], w_lo[:, :H])
        l2[at, :] = product(raw_r[at, :], w_hi[:, H:], w_lo[:, H:])
        cross_part(at)
        return carry

    lax.fori_loop(0, RAW // CHUNK, raw_part, 0)

    def late_part(i, carry):
        arrived(u2.at[late(i)], r_recv.at[i, 0])
        arrived(l2.at[late(i)], r_recv.at[i, 1])
        cross_part(late(i))
        return carry

    lax.fori_loop(0, n_turn, late_part, 0)
    part2[...] = (acc2[:H, :H] + acc2[H:, H:]) + (acc2[:H, H:] + acc2[H:, :H])
    side = buf_0.shape[1]
    place = (lax.rem(row, side), row // side)

    def exchange(phase, half, k, src):
        axis = (phase + half) % 2
        there = lax.rem(place[axis] + k, side)
        peer = place[1] * side + there if axis == 0 else there * side + place[0]
        buf = buf_1 if phase else buf_0
        return pltpu.make_async_remote_copy(
            src, buf.at[half, place[axis]],
            s2_send.at[phase, half, k], s2_recv.at[phase, half, k],
            device_id={"row": peer}, device_id_type=MESH,
        )

    def half_of(half):
        return pl.ds(half * (H // 2), H // 2)

    order = [side // 2] + [k for k in range(1, side) if k != side // 2]
    sent_0 = [[exchange(0, h, k, part2.at[half_of(h)]) for k in order] for h in range(2)]
    for pair in zip(*sent_0):
        for copy in pair:
            copy.start()
    sent_1 = []
    for h in range(2):
        buf_0[h, place[h]] = part2[half_of(h), :]
        for copy in sent_0[h]:
            copy.wait_recv()
        buf_1[h, place[1 - h]] = sum_of([buf_0[h, k] for k in range(side)])
        sent_1.append([exchange(1, h, k, buf_1.at[h, place[1 - h]]) for k in order])
        for copy in sent_1[h]:
            copy.start()
    for h in range(2):
        for copy in sent_1[h]:
            copy.wait_recv()
        total2[half_of(h), :] = sum_of([buf_1[h, k] for k in range(side)])
    out_c = pltpu.make_async_copy(total2, c_out, load_sem.at[0])
    out_c.start()

    right_sent(raw_src, raw_send.at[0])
    left_sent(raw_src, raw_send.at[1])
    right_sent(pack_send.at[0, mine], pack_ssem.at[0])
    left_sent(pack_send.at[1, mine], pack_ssem.at[1])
    for o in range(1, n_row):
        pass_on(o).wait_send()
    for h in range(2):
        for copy in sent_0[h] + sent_1[h]:
            copy.wait_send()

    def drain(i, carry):
        right_sent(send_r.at[sent(i)], r_send.at[i])
        left_sent(send_x.at[sent(i)], x_send.at[i])
        return carry

    lax.fori_loop(0, n_turn, drain, 0)

    def written(i, carry):
        at = pl.ds(pl.multiple_of(i * CHUNK, 8), CHUNK)
        pltpu.make_async_copy(u2.at[at], u_out.at[at], out_sem.at[0, i]).wait()
        pltpu.make_async_copy(l2.at[at], l_out.at[at], out_sem.at[1, i]).wait()
        return carry

    lax.fori_loop(0, rows // CHUNK, written, 0)
    out_pack.wait()
    out_c.wait()


def first_round(n_col, n_row, snapshots, orientation):
    rows = snapshots.shape[0]
    late = rows - RAW
    n_turn = late // CHUNK
    side = 4 if n_row == 16 else 2
    sem = pltpu.SemaphoreType.DMA
    any_spec = pl.BlockSpec(memory_space=pl.ANY)
    return pl.pallas_call(
        functools.partial(first_kernel, n_col, n_row),
        out_shape=[
            jax.ShapeDtypeStruct((rows, H), F32),
            jax.ShapeDtypeStruct((rows, H), F32),
            jax.ShapeDtypeStruct((2, 3 * H, H), F32),
            jax.ShapeDtypeStruct((H, H), F32),
        ],
        in_specs=[any_spec] * 2,
        out_specs=[any_spec] * 4,
        scratch_shapes=[
            pltpu.VMEM((rows, 2 * H), F32),
            pltpu.VMEM((RAW, 2 * H), F32),
            pltpu.VMEM((RAW, 2 * H), F32),
            pltpu.VMEM((rows, H), F32),
            pltpu.VMEM((rows, H), F32),
            pltpu.VMEM((late, H), F32),
            pltpu.VMEM((late, H), F32),
            pltpu.VMEM((2 * H, 4 * H), F32),
            pltpu.VMEM((3 * H, H), F32),
            pltpu.VMEM((n_row, 3 * H // n_row, H), F32),
            pltpu.VMEM((3 * H, H), F32),
            pltpu.VMEM((2, 10, H + 2 * PAD, H), F32),
            pltpu.VMEM((2, 3 * H, H), F32),
            pltpu.VMEM((2, 3 * H, H), F32),
            pltpu.VMEM((2 * H, 2 * H), BF16),
            pltpu.VMEM((2 * H, 2 * H), BF16),
            pltpu.VMEM((2 * H, 2 * H), F32),
            pltpu.VMEM((H, H), F32),
            pltpu.VMEM((2, side, H // 2, H), F32),
            pltpu.VMEM((2, side, H // 2, H), F32),
            pltpu.VMEM((H, H), F32),
            pltpu.SMEM(orientation.shape, jnp.int32),
            sem((8,)),
            sem((n_row,)), sem((n_row,)), sem((n_row,)), sem((n_row,)),
            sem((2, 2, side)), sem((2, 2, side)), sem((n_row,)), sem((n_row,)),
            sem((2,)), sem((2,)), sem((2,)), sem((2,)),
            sem((n_turn,)), sem((n_turn, 2)), sem((n_turn,)),
            sem((2, rows // CHUNK + 1)),
        ],
        compiler_params=pltpu.CompilerParams(
            collective_id=0, has_side_effects=True, vmem_limit_bytes=48 * 2**20
        ),
    )(snapshots, orientation)


def last_kernel(
    n_col,
    u_ref, l_ref, pack_ref, c_ref, ori_ref,
    out_ref, basis_ref,
    u, l, pack, c, ori, out, basis, state, w_hi, w_lo, load_sem, out_sem,
):
    rows = u.shape[0]
    col = lax.axis_index("col")
    row = lax.axis_index("row")
    refs = (c_ref, ori_ref, pack_ref, u_ref, l_ref)
    loads = [
        pltpu.make_async_copy(src, dst, load_sem.at[i])
        for i, (src, dst) in enumerate(zip(refs, (c, ori, pack, u, l)))
    ]
    for copy in loads:
        copy.start()
    for copy in loads[:3]:
        copy.wait()
    flipped = ori[1, col] == 1
    jacobi(state, pack[0, 2 * H :], c[...], pack[1, 2 * H :], flipped)
    up, lo = rotation(state, flipped)
    hi, lo = split(jnp.concatenate([up, lo], 1))
    w_hi[...] = hi
    w_lo[...] = lo
    for copy in loads[3:]:
        copy.wait()

    def finish(i):
        at = pl.ds(i * OUT_CHUNK, OUT_CHUNK)
        return pltpu.make_async_copy(out.at[at], out_ref.at[at], out_sem.at[i])

    for i in range(rows // OUT_CHUNK):
        at = pl.ds(i * OUT_CHUNK, OUT_CHUNK)
        joined = jnp.concatenate([u[at, :], l[at, :]], 1)
        out[at, :] = product(joined, w_hi[...], w_lo[...])
        finish(i).start()

    group = row // 2
    lower_half = row % 2 == 1
    sides = []
    for side, source in ((0, jnp.maximum(col - 1, 0)), (1, jnp.minimum(col + 1, n_col - 1))):
        part = jnp.where(lower_half, pack[side, H : 2 * H], pack[side, :H])
        sides.append(jnp.where(group == source, part, 0.0))
    basis[...] = product(jnp.concatenate(sides, 1), w_hi[...], w_lo[...])
    out_basis = pltpu.make_async_copy(basis, basis_ref, load_sem.at[0])
    out_basis.start()
    for i in range(rows // OUT_CHUNK):
        finish(i).wait()
    out_basis.wait()


def last_round(n_col, n_row, u2, l2, pack, cross, orientation):
    rows = u2.shape[0]
    basis_rows = 2 * H * n_col // n_row
    sem = pltpu.SemaphoreType.DMA
    any_spec = pl.BlockSpec(memory_space=pl.ANY)
    return pl.pallas_call(
        functools.partial(last_kernel, n_col),
        out_shape=[
            jax.ShapeDtypeStruct((rows, 2 * H), F32),
            jax.ShapeDtypeStruct((basis_rows, 2 * H), F32),
        ],
        in_specs=[any_spec] * 5,
        out_specs=[any_spec] * 2,
        scratch_shapes=[
            pltpu.VMEM((rows, H), F32),
            pltpu.VMEM((rows, H), F32),
            pltpu.VMEM((2, 3 * H, H), F32),
            pltpu.VMEM((H, H), F32),
            pltpu.SMEM(orientation.shape, jnp.int32),
            pltpu.VMEM((rows, 2 * H), F32),
            pltpu.VMEM((basis_rows, 2 * H), F32),
            pltpu.VMEM((2, 10, H + 2 * PAD, H), F32),
            pltpu.VMEM((2 * H, 2 * H), BF16),
            pltpu.VMEM((2 * H, 2 * H), BF16),
            sem((5,)),
            sem((rows // OUT_CHUNK,)),
        ],
        compiler_params=pltpu.CompilerParams(vmem_limit_bytes=32 * 2**20),
    )(u2, l2, pack, cross, orientation)


def on_device(n_col, n_row, snapshots, orientation):
    moved = first_round(n_col, n_row, snapshots, orientation)
    return tuple(last_round(n_col, n_row, *moved, orientation))


def solution(mesh):
    return jax.shard_map(
        functools.partial(on_device, mesh.shape["col"], mesh.shape["row"]),
        mesh=mesh,
        in_specs=(P("row", "col"), P()),
        out_specs=(P("row", "col"), P("row", "col")),
        check_vma=False,
    )
```

time: 73.4 us -> 65.8 us (0.90)
  the two profiles are of different devices: /device:TPU:1 before, /device:TPU:0 now
where the time goes in v2:
time: 65.8 us; the launch traced here: 65.7 us
  Pallas kernels  64.4 us (98%)
  local copies, waits for them, and re-layouts  0.67 us (1%)
    pallas_call x1, Pallas kernels, first_round(): pl.pallas_call(functools.partial(first_kernel, n_col, n_row), out_shape=[...  56.6 us
    pallas_call x1, Pallas kernels, last_round(): pl.pallas_call(functools.partial(last_kernel, n_col), out_shape=[jax.Shap...  7.79 us

profile of v2, /device:TPU:0, one launch (start us, length us, event | category | flops | bytes accessed | tf_op | source)
XLA Modules:
  0.0 65.7 jit_solution(13177924894443472393)
XLA Ops:
  0.6 0.0 copy-start
  0.6 0.7 %copy-done = s32[2,8]{1,0:T(2,128)S(1)} copy-done((s32[2,8]{1,0:T(2,128)S(1)}, s32[2,8]{1,0:T(2,128)}, u32[]{:S(2)}) %copy-start) | copy-done | bytes 88
  1.3 56.6 %shard_map.41 = (f32[4096,128]{1,0:T(8,128)S(1)}, f32[4096,128]{1,0:T(8,128)S(1)}, f32[2,384,128]{2,1,0:T(8,128)S(1)}, f32[128,128]{1,0:T(8,128)S(1)}) custom-call(f32[4096,256]{1,0:T(8,128)} %x_ref.1, s32[2,8]{1,0:T(2,128)S(1)} %copy-done), custom_call_target="tpu_custom_call" | custom-call | tf_op jit(solution)/shard_map/pallas_call | solution.py:431
  57.9 7.8 %shard_map.42 = (f32[4096,256]{1,0:T(8,128)}, f32[128,256]{1,0:T(8,128)}) custom-call(f32[4096,128]{1,0:T(8,128)S(1)} %get-tuple-element.6.u_ref, f32[4096,128]{1,0:T(8,128)S(1)} %get-tuple-element.7.l_ref, f32[2,384,128]{2,1,0:T(8,128)S(1)} %get-tuple-element.8.pack_ref, f32[128,128]{1,0:T(8,128)S(1)} %get-tuple-element.9.c_ref, s32[2,8]{1,0:T(2,128)S(1)} %copy-done), custom_call_target="tpu_custom_call" | custom-call | tf_op jit(solution)/shard_map/pallas_call | solution.py:533
Async XLA Ops:
  0.6 0.7 %copy-start = (s32[2,8]{1,0:T(2,128)S(1)}, s32[2,8]{1,0:T(2,128)}, u32[]{:S(2)}) copy-start(s32[2,8]{1,0:T(2,128)} %ori_ref.3) | copy-start | bytes 196

commit v3 on v2

--- a/solution.py
+++ b/solution.py
@@ -12,11 +12,15 @@
 F32 = jnp.float32
 BF16 = jnp.bfloat16
 MESH = pl.DeviceIdType.MESH
-RAW = 1280
+RAW = 1536
 CHUNK = 256
 OUT_CHUNK = 512
+RAW_CHUNK = 256
+HEAD = 1
+EARLY = 4
 PAD = 8
 UNROLL = 8
+LAST_UNROLL = 24
 SQRT_HALF = 0.5**0.5
 
 
@@ -34,7 +38,7 @@
     return cc * half, ss * half, (ss * (q * q)) * d
 
 
-def jacobi(state, a, c, d, flipped):
+def jacobi(state, a, c, d, flipped, unroll):
     lane = lax.broadcasted_iota(jnp.int32, (H, H), 1)
     row = lax.broadcasted_iota(jnp.int32, (H, H), 0)
     eye = (lane == row).astype(F32)
@@ -82,12 +86,12 @@
             put(dst, 4, i, u[4] - shift, l[4] + shift)
 
     def several(_, carry):
-        for _ in range(UNROLL // 2):
+        for _ in range(unroll // 2):
             step(0, 1)
             step(1, 0)
         return carry
 
-    lax.fori_loop(0, STEPS // UNROLL, several, 0)
+    lax.fori_loop(0, STEPS // unroll, several, 0)
 
 
 def final_gram(state, k):
@@ -135,6 +139,12 @@
     return terms[0]
 
 
+def thin_product(x, w_both, w_hi):
+    hi, lo = split(x)
+    both = dot(hi, w_both)
+    return both[:, :H] + (both[:, H:] + dot(lo, w_hi))
+
+
 def product(x, w_hi, w_lo):
     hi, lo = split(x)
     return dot(hi, w_hi) + (dot(hi, w_lo) + dot(lo, w_hi))
@@ -143,11 +153,11 @@
 def first_kernel(
     n_col, n_row,
     x_ref, ori_ref,
-    u_out, l_out, pack_out, c_out,
-    b, raw_l, raw_r, u2, l2, send_r, send_x, acc, part, rs_buf, total, state,
-    pack_send, pack, w_hi, w_lo, acc2, part2, buf_0, buf_1, total2, ori,
+    u2, l2, pack, total2,
+    b, raw_l, raw_r, send_r, send_x, acc, part, rs_buf, total, state,
+    pack_send, w_hi, w_lo, v_hi, v_lo, acc2, part2, buf_0, buf_1, ori,
     load_sem, rs_send, rs_recv, ag_send, ag_recv, s2_send, s2_recv, pag_send, pag_recv,
-    raw_send, raw_recv, pack_ssem, pack_rsem, r_send, r_recv, x_send, out_sem,
+    raw_send, raw_recv, pack_ssem, pack_rsem, r_send, r_recv, x_send, ori_sem,
 ):
     rows = b.shape[0]
     col = lax.axis_index("col")
@@ -158,12 +168,12 @@
     left = lax.rem(col + n_col - 1, n_col)
 
     barrier = pltpu.get_barrier_semaphore()
+    for side in (left, right):
+        pl.semaphore_signal(barrier, inc=1, device_id={"col": side}, device_id_type=MESH)
     for o in range(1, n_row):
         pl.semaphore_signal(
             barrier, inc=1, device_id={"row": lax.rem(row + o, n_row)}, device_id_type=MESH
         )
-    for side in (left, right):
-        pl.semaphore_signal(barrier, inc=1, device_id={"col": side}, device_id_type=MESH)
 
     n_load = load_sem.shape[0]
     step = rows // n_load
@@ -174,7 +184,7 @@
 
     for i in range(n_load):
         load(i).start()
-    get_ori = pltpu.make_async_copy(ori_ref, ori, out_sem.at[0, rows // CHUNK])
+    get_ori = pltpu.make_async_copy(ori_ref, ori, ori_sem.at[0])
     get_ori.start()
 
     def right_start(src, dst, ssem, rsem):
@@ -268,11 +278,34 @@
 
     get_ori.wait()
     flipped = ori[0, col] == 1
-    jacobi(state, total[:H], total[H : 2 * H], total[2 * H :], flipped)
+    jacobi(state, total[:H], total[H : 2 * H], total[2 * H :], flipped, UNROLL)
     up, lo = rotation(state, flipped)
-    gram_up, gram_lo = final_gram(state, 0), final_gram(state, 5)
     w_r = jnp.where(first, lo, up)
     w_x = jnp.where(first, up, lo)
+    hi, low = split(jnp.concatenate([w_r, w_x], 1))
+    w_hi[...] = hi
+    w_lo[...] = low
+
+    n_turn = (rows - RAW) // CHUNK
+
+    def late(i):
+        return pl.ds(pl.multiple_of(RAW + i * CHUNK, 8), CHUNK)
+
+    def sent(i):
+        return pl.ds(pl.multiple_of(i * CHUNK, 8), CHUNK)
+
+    def turn_part(i, carry):
+        turned = product(b[late(i), :], w_hi[...], w_lo[...])
+        send_r[sent(i), :] = turned[:, :H]
+        send_x[sent(i), :] = turned[:, H:]
+        dst = (u2.at[late(i)], l2.at[late(i)])
+        right_start(send_r.at[sent(i)], dst, r_send.at[i], r_recv.at[i])
+        left_start(send_x.at[sent(i)], dst, x_send.at[i], r_recv.at[i])
+        return carry
+
+    lax.fori_loop(0, HEAD, turn_part, 0)
+
+    gram_up, gram_lo = final_gram(state, 0), final_gram(state, 5)
     pack_send[0, : 2 * H] = w_r
     pack_send[0, 2 * H :] = jnp.where(first, gram_lo, gram_up)
     pack_send[1, : 2 * H] = w_x
@@ -282,40 +315,23 @@
     pack_dst = (pack.at[0, mine], pack.at[1, mine])
     right_start(pack_send.at[0, mine], pack_dst, pack_ssem.at[0], pack_rsem)
     left_start(pack_send.at[1, mine], pack_dst, pack_ssem.at[1], pack_rsem)
-    hi, lo = split(jnp.concatenate([w_r, w_x], 1))
-    w_hi[...] = hi
-    w_lo[...] = lo
-
-    n_turn = (rows - RAW) // CHUNK
-
-    def late(i):
-        return pl.ds(pl.multiple_of(RAW + i * CHUNK, 8), CHUNK)
-
-    def sent(i):
-        return pl.ds(pl.multiple_of(i * CHUNK, 8), CHUNK)
-
-    def turn_part(i, carry):
-        turned = product(b[late(i), :], w_hi[...], w_lo[...])
-        send_r[sent(i), :] = turned[:, :H]
-        send_x[sent(i), :] = turned[:, H:]
-        dst = (u2.at[late(i)], l2.at[late(i)])
-        right_start(send_r.at[sent(i)], dst, r_send.at[i], r_recv.at[i])
-        left_start(send_x.at[sent(i)], dst, x_send.at[i], r_recv.at[i])
-        return carry
-
-    lax.fori_loop(0, n_turn, turn_part, 0)
+
+    lax.fori_loop(HEAD, n_turn, turn_part, 0)
 
     acc2[...] = jnp.zeros_like(acc2)
 
-    def cross_part(at):
-        u_hi, u_lo = split(u2[at, :])
-        l_hi, l_lo = split(l2[at, :])
+    def cross_part(u, l):
+        u_hi, u_lo = split(u)
+        l_hi, l_lo = split(l)
         acc2[...] += dot_t(
             jnp.concatenate([u_hi, u_lo], 1), jnp.concatenate([l_hi, l_lo], 1)
         )
-        slot = at.start // CHUNK
-        pltpu.make_async_copy(u2.at[at], u_out.at[at], out_sem.at[0, slot]).start()
-        pltpu.make_async_copy(l2.at[at], l_out.at[at], out_sem.at[1, slot]).start()
+
+    def late_part(i, carry):
+        arrived(u2.at[late(i)], r_recv.at[i, 0])
+        arrived(l2.at[late(i)], r_recv.at[i, 1])
+        cross_part(u2[late(i), :], l2[late(i), :])
+        return carry
 
     def pass_on(o):
         return pltpu.make_async_remote_copy(
@@ -329,31 +345,25 @@
         pass_on(o).start()
     arrived(raw_l, raw_recv.at[0])
     arrived(raw_r, raw_recv.at[1])
+    lax.fori_loop(0, EARLY, late_part, 0)
     for o in range(1, n_row):
         pass_on(o).wait_recv()
-    out_pack = pltpu.make_async_copy(pack, pack_out, out_sem.at[1, rows // CHUNK])
-    out_pack.start()
-    wl_hi, wl_lo = split(pack[0, : 2 * H])
-    wr_hi, wr_lo = split(pack[1, : 2 * H])
-    w_hi[...] = jnp.concatenate([wl_hi, wr_hi], 1)
-    w_lo[...] = jnp.concatenate([wl_lo, wr_lo], 1)
+    for side, (whole, part_hi) in enumerate(((w_hi, v_hi), (w_lo, v_lo))):
+        hi, low = split(pack[side, : 2 * H])
+        whole[...] = jnp.concatenate([hi, low], 1)
+        part_hi[...] = hi
 
     def raw_part(i, carry):
-        at = pl.ds(pl.multiple_of(i * CHUNK, 8), CHUNK)
-        u2[at, :] = product(raw_l[at, :], w_hi[:, :H], w_lo[:, :H])
-        l2[at, :] = product(raw_r[at, :], w_hi[:, H:], w_lo[:, H:])
-        cross_part(at)
+        at = pl.ds(pl.multiple_of(i * RAW_CHUNK, 8), RAW_CHUNK)
+        u = thin_product(raw_l[at, :], w_hi[...], v_hi[...])
+        l = thin_product(raw_r[at, :], w_lo[...], v_lo[...])
+        u2[at, :] = u
+        l2[at, :] = l
+        cross_part(u, l)
         return carry
 
-    lax.fori_loop(0, RAW // CHUNK, raw_part, 0)
-
-    def late_part(i, carry):
-        arrived(u2.at[late(i)], r_recv.at[i, 0])
-        arrived(l2.at[late(i)], r_recv.at[i, 1])
-        cross_part(late(i))
-        return carry
-
-    lax.fori_loop(0, n_turn, late_part, 0)
+    lax.fori_loop(0, RAW // RAW_CHUNK, raw_part, 0)
+    lax.fori_loop(EARLY, n_turn, late_part, 0)
     part2[...] = (acc2[:H, :H] + acc2[H:, H:]) + (acc2[:H, H:] + acc2[H:, :H])
     side = buf_0.shape[1]
     place = (lax.rem(row, side), row // side)
@@ -390,9 +400,6 @@
         for copy in sent_1[h]:
             copy.wait_recv()
         total2[half_of(h), :] = sum_of([buf_1[h, k] for k in range(side)])
-    out_c = pltpu.make_async_copy(total2, c_out, load_sem.at[0])
-    out_c.start()
-
     right_sent(raw_src, raw_send.at[0])
     left_sent(raw_src, raw_send.at[1])
     right_sent(pack_send.at[0, mine], pack_ssem.at[0])
@@ -410,16 +417,6 @@
 
     lax.fori_loop(0, n_turn, drain, 0)
 
-    def written(i, carry):
-        at = pl.ds(pl.multiple_of(i * CHUNK, 8), CHUNK)
-        pltpu.make_async_copy(u2.at[at], u_out.at[at], out_sem.at[0, i]).wait()
-        pltpu.make_async_copy(l2.at[at], l_out.at[at], out_sem.at[1, i]).wait()
-        return carry
-
-    lax.fori_loop(0, rows // CHUNK, written, 0)
-    out_pack.wait()
-    out_c.wait()
-
 
 def first_round(n_col, n_row, snapshots, orientation):
     rows = snapshots.shape[0]
@@ -427,7 +424,6 @@
     n_turn = late // CHUNK
     side = 4 if n_row == 16 else 2
     sem = pltpu.SemaphoreType.DMA
-    any_spec = pl.BlockSpec(memory_space=pl.ANY)
     return pl.pallas_call(
         functools.partial(first_kernel, n_col, n_row),
         out_shape=[
@@ -436,14 +432,12 @@
             jax.ShapeDtypeStruct((2, 3 * H, H), F32),
             jax.ShapeDtypeStruct((H, H), F32),
         ],
-        in_specs=[any_spec] * 2,
-        out_specs=[any_spec] * 4,
+        in_specs=[pl.BlockSpec(memory_space=pltpu.HBM)] * 2,
+        out_specs=[pl.BlockSpec(memory_space=pltpu.VMEM)] * 4,
         scratch_shapes=[
             pltpu.VMEM((rows, 2 * H), F32),
             pltpu.VMEM((RAW, 2 * H), F32),
             pltpu.VMEM((RAW, 2 * H), F32),
-            pltpu.VMEM((rows, H), F32),
-            pltpu.VMEM((rows, H), F32),
             pltpu.VMEM((late, H), F32),
             pltpu.VMEM((late, H), F32),
             pltpu.VMEM((2 * H, 4 * H), F32),
@@ -452,21 +446,21 @@
             pltpu.VMEM((3 * H, H), F32),
             pltpu.VMEM((2, 10, H + 2 * PAD, H), F32),
             pltpu.VMEM((2, 3 * H, H), F32),
-            pltpu.VMEM((2, 3 * H, H), F32),
             pltpu.VMEM((2 * H, 2 * H), BF16),
             pltpu.VMEM((2 * H, 2 * H), BF16),
+            pltpu.VMEM((2 * H, H), BF16),
+            pltpu.VMEM((2 * H, H), BF16),
             pltpu.VMEM((2 * H, 2 * H), F32),
             pltpu.VMEM((H, H), F32),
             pltpu.VMEM((2, side, H // 2, H), F32),
             pltpu.VMEM((2, side, H // 2, H), F32),
-            pltpu.VMEM((H, H), F32),
             pltpu.SMEM(orientation.shape, jnp.int32),
-            sem((8,)),
+            sem((4,)),
             sem((n_row,)), sem((n_row,)), sem((n_row,)), sem((n_row,)),
             sem((2, 2, side)), sem((2, 2, side)), sem((n_row,)), sem((n_row,)),
             sem((2,)), sem((2,)), sem((2,)), sem((2,)),
             sem((n_turn,)), sem((n_turn, 2)), sem((n_turn,)),
-            sem((2, rows // CHUNK + 1)),
+            sem((1,)),
         ],
         compiler_params=pltpu.CompilerParams(
             collective_id=0, has_side_effects=True, vmem_limit_bytes=48 * 2**20
@@ -476,30 +470,22 @@
 
 def last_kernel(
     n_col,
-    u_ref, l_ref, pack_ref, c_ref, ori_ref,
+    u, l, pack, c, ori_ref,
     out_ref, basis_ref,
-    u, l, pack, c, ori, out, basis, state, w_hi, w_lo, load_sem, out_sem,
+    ori, out, basis, state, w_hi, w_lo, ori_sem, out_sem,
 ):
     rows = u.shape[0]
     col = lax.axis_index("col")
     row = lax.axis_index("row")
-    refs = (c_ref, ori_ref, pack_ref, u_ref, l_ref)
-    loads = [
-        pltpu.make_async_copy(src, dst, load_sem.at[i])
-        for i, (src, dst) in enumerate(zip(refs, (c, ori, pack, u, l)))
-    ]
-    for copy in loads:
-        copy.start()
-    for copy in loads[:3]:
-        copy.wait()
+    get_ori = pltpu.make_async_copy(ori_ref, ori, ori_sem.at[0])
+    get_ori.start()
+    get_ori.wait()
     flipped = ori[1, col] == 1
-    jacobi(state, pack[0, 2 * H :], c[...], pack[1, 2 * H :], flipped)
+    jacobi(state, pack[0, 2 * H :], c[...], pack[1, 2 * H :], flipped, LAST_UNROLL)
     up, lo = rotation(state, flipped)
     hi, lo = split(jnp.concatenate([up, lo], 1))
     w_hi[...] = hi
     w_lo[...] = lo
-    for copy in loads[3:]:
-        copy.wait()
 
     def finish(i):
         at = pl.ds(i * OUT_CHUNK, OUT_CHUNK)
@@ -518,7 +504,7 @@
         part = jnp.where(lower_half, pack[side, H : 2 * H], pack[side, :H])
         sides.append(jnp.where(group == source, part, 0.0))
     basis[...] = product(jnp.concatenate(sides, 1), w_hi[...], w_lo[...])
-    out_basis = pltpu.make_async_copy(basis, basis_ref, load_sem.at[0])
+    out_basis = pltpu.make_async_copy(basis, basis_ref, ori_sem.at[0])
     out_basis.start()
     for i in range(rows // OUT_CHUNK):
         finish(i).wait()
@@ -529,34 +515,32 @@
     rows = u2.shape[0]
     basis_rows = 2 * H * n_col // n_row
     sem = pltpu.SemaphoreType.DMA
-    any_spec = pl.BlockSpec(memory_space=pl.ANY)
+    hbm = pl.BlockSpec(memory_space=pltpu.HBM)
     return pl.pallas_call(
         functools.partial(last_kernel, n_col),
         out_shape=[
             jax.ShapeDtypeStruct((rows, 2 * H), F32),
             jax.ShapeDtypeStruct((basis_rows, 2 * H), F32),
         ],
-        in_specs=[any_spec] * 5,
-        out_specs=[any_spec] * 2,
+        in_specs=[pl.BlockSpec(memory_space=pltpu.VMEM)] * 4 + [hbm],
+        out_specs=[hbm] * 2,
         scratch_shapes=[
-            pltpu.VMEM((rows, H), F32),
-            pltpu.VMEM((rows, H), F32),
-            pltpu.VMEM((2, 3 * H, H), F32),
-            pltpu.VMEM((H, H), F32),
             pltpu.SMEM(orientation.shape, jnp.int32),
             pltpu.VMEM((rows, 2 * H), F32),
             pltpu.VMEM((basis_rows, 2 * H), F32),
             pltpu.VMEM((2, 10, H + 2 * PAD, H), F32),
             pltpu.VMEM((2 * H, 2 * H), BF16),
             pltpu.VMEM((2 * H, 2 * H), BF16),
-            sem((5,)),
+            sem((1,)),
             sem((rows // OUT_CHUNK,)),
         ],
-        compiler_params=pltpu.CompilerParams(vmem_limit_bytes=32 * 2**20),
+        compiler_params=pltpu.CompilerParams(vmem_limit_bytes=48 * 2**20),
     )(u2, l2, pack, cross, orientation)
 
 
 def on_device(n_col, n_row, snapshots, orientation):
+    snapshots = pltpu.with_memory_space_constraint(snapshots, pltpu.HBM)
+    orientation = pltpu.with_memory_space_constraint(orientation, pltpu.HBM)
     moved = first_round(n_col, n_row, snapshots, orientation)
     return tuple(last_round(n_col, n_row, *moved, orientation))
 

time: 65.8 us -> 58.5 us (0.89)
  the two profiles are of different devices: /device:TPU:0 before, /device:TPU:1 now
where the time goes in v3:
time: 58.5 us; the launch traced here: 58.4 us
  Pallas kernels  57.8 us (99%)
  between operations  0.64 us (1%)
    pallas_call x1, Pallas kernels, first_round(): pl.pallas_call(functools.partial(first_kernel, n_col, n_row), out_shape=[...  50.2 us
    pallas_call x1, Pallas kernels, last_round(): pl.pallas_call(functools.partial(last_kernel, n_col), out_shape=[jax.Shap...  7.58 us

profile of v3, /device:TPU:1, one launch (start us, length us, event | category | flops | bytes accessed | tf_op | source)
XLA Modules:
  0.0 58.4 jit_solution(14552139288916370389)
XLA Ops:
  0.6 50.2 %shard_map.41 = (f32[4096,128]{1,0:T(8,128)S(1)}, f32[4096,128]{1,0:T(8,128)S(1)}, f32[2,384,128]{2,1,0:T(8,128)S(1)}, f32[128,128]{1,0:T(8,128)S(1)}) custom-call(f32[4096,256]{1,0:T(8,128)} %x_ref.1, s32[2,8]{1,0:T(2,128)} %ori_ref.3), custom_call_target="tpu_custom_call" | custom-call | tf_op jit(solution)/shard_map/pallas_call | solution.py:427
  50.8 7.6 %shard_map.42 = (f32[4096,256]{1,0:T(8,128)}, f32[128,256]{1,0:T(8,128)}) custom-call(f32[4096,128]{1,0:T(8,128)S(1)} %get-tuple-element.6.u, f32[4096,128]{1,0:T(8,128)S(1)} %get-tuple-element.7.l, f32[2,384,128]{2,1,0:T(8,128)S(1)} %get-tuple-element.8.pack, f32[128,128]{1,0:T(8,128)S(1)} %get-tuple-element.9.c, s32[2,8]{1,0:T(2,128)} %ori_ref.3), custom_call_target="tpu_custom_call" | custom-call | tf_op jit(solution)/shard_map/pallas_call | solution.py:519

commit v4 on v3

--- a/solution.py
+++ b/solution.py
@@ -12,30 +12,29 @@
 F32 = jnp.float32
 BF16 = jnp.bfloat16
 MESH = pl.DeviceIdType.MESH
-RAW = 1536
-CHUNK = 256
+RAW = 1408
+CHUNK = 384
 OUT_CHUNK = 512
-RAW_CHUNK = 256
+RAW_CHUNK = 352
 HEAD = 1
-EARLY = 4
+EARLY = 3
 PAD = 8
 UNROLL = 8
 LAST_UNROLL = 24
 SQRT_HALF = 0.5**0.5
-
-
-def angles(a, b, d):
+TOP = 2.0**61
+FLOOR = 2.0**-62
+
+
+def angles(a, b, d, scale):
     e = b - a
-    scale = pltpu.reciprocal(jnp.maximum(jnp.abs(e), jnp.abs(d)), approx=True)
-    scale = jnp.where(e >= 0.0, scale, -scale)
-    e = e * scale
-    dd = (d + d) * scale
-    r = lax.rsqrt(e * e + dd * dd)
-    cc = e * r + 1.0
-    q = lax.rsqrt(cc)
-    ss = dd * r
-    half = q * SQRT_HALF
-    return cc * half, ss * half, (ss * (q * q)) * d
+    size = jnp.abs(e) + FLOOR
+    ds = d * jnp.where(e >= 0.0, scale, -scale)
+    r = lax.rsqrt(size * size + ds * ds)
+    cc = size * r + 1.0
+    half = lax.rsqrt(cc) * SQRT_HALF
+    s = (ds * r) * half
+    return cc * half, s, (s * half) * (d * scale)
 
 
 def jacobi(state, a, c, d, flipped, unroll):
@@ -46,17 +45,22 @@
     ct = jnp.transpose(c)
     upper = jnp.where(flipped, d, a)
     lower = jnp.where(flipped, a, d)
+    half_a = 0.5 * jnp.sum(upper * eye, axis=1, keepdims=True)
+    half_b = 0.5 * jnp.sum(lower * eye, axis=1, keepdims=True)
+    total = jnp.sum(half_a + half_b, axis=0, keepdims=True)
+    scale = TOP / jnp.maximum(total, 1.0 / TOP)
     held = slice(PAD, PAD + H)
     state[0, 0, held] = upper
     state[0, 1, held] = jnp.where(flipped, ct, c)
     state[0, 2, held] = eye
     state[0, 3, held] = zero
-    state[0, 4, held] = jnp.broadcast_to(jnp.sum(upper * eye, axis=1, keepdims=True), (H, H))
+    state[0, 4, held] = jnp.broadcast_to(half_a * scale, (H, H))
     state[0, 5, held] = jnp.where(flipped, c, ct)
     state[0, 6, held] = lower
     state[0, 7, held] = zero
     state[0, 8, held] = eye
-    state[0, 9, held] = jnp.broadcast_to(jnp.sum(lower * eye, axis=1, keepdims=True), (H, H))
+    state[0, 9, held] = jnp.broadcast_to(half_b * scale, (H, H))
+    scale = jnp.broadcast_to(scale, (8, H))
 
     def put(dst, k, i, f, g):
         r = PAD + 8 * i
@@ -80,7 +84,7 @@
             l = [state[src, k + 5, r] for k in range(5)]
             dot_ul = jnp.sum(u[2] * l[0] + u[3] * l[1], axis=1, keepdims=True)
             dot_ul = jnp.broadcast_to(dot_ul, (8, H))
-            cos, sin, shift = angles(u[4], l[4], dot_ul)
+            cos, sin, shift = angles(u[4], l[4], dot_ul, scale)
             for k in range(4):
                 put(dst, k, i, u[k] * cos - l[k] * sin, u[k] * sin + l[k] * cos)
             put(dst, 4, i, u[4] - shift, l[4] + shift)
@@ -270,11 +274,9 @@
             gather(o).start()
         for o in range(1, n_row):
             gather(o).wait_recv()
-        for o in range(1, n_row):
-            scatter(o).wait_send()
-            gather(o).wait_send()
-
-    all_reduce(part, rs_buf, total, rs_send, rs_recv, ag_send, ag_recv)
+        return [make(o) for make in (scatter, gather) for o in range(1, n_row)]
+
+    sums_sent = all_reduce(part, rs_buf, total, rs_send, rs_recv, ag_send, ag_recv)
 
     get_ori.wait()
     flipped = ori[0, col] == 1
@@ -387,6 +389,21 @@
     for pair in zip(*sent_0):
         for copy in pair:
             copy.start()
+    for copy in sums_sent:
+        copy.wait_send()
+    right_sent(raw_src, raw_send.at[0])
+    left_sent(raw_src, raw_send.at[1])
+    right_sent(pack_send.at[0, mine], pack_ssem.at[0])
+    left_sent(pack_send.at[1, mine], pack_ssem.at[1])
+    for o in range(1, n_row):
+        pass_on(o).wait_send()
+    def drain(i, carry):
+        right_sent(send_r.at[sent(i)], r_send.at[i])
+        left_sent(send_x.at[sent(i)], x_send.at[i])
+        return carry
+
+    lax.fori_loop(0, n_turn, drain, 0)
+
     sent_1 = []
     for h in range(2):
         buf_0[h, place[h]] = part2[half_of(h), :]
@@ -400,22 +417,9 @@
         for copy in sent_1[h]:
             copy.wait_recv()
         total2[half_of(h), :] = sum_of([buf_1[h, k] for k in range(side)])
-    right_sent(raw_src, raw_send.at[0])
-    left_sent(raw_src, raw_send.at[1])
-    right_sent(pack_send.at[0, mine], pack_ssem.at[0])
-    left_sent(pack_send.at[1, mine], pack_ssem.at[1])
-    for o in range(1, n_row):
-        pass_on(o).wait_send()
     for h in range(2):
         for copy in sent_0[h] + sent_1[h]:
             copy.wait_send()
-
-    def drain(i, carry):
-        right_sent(send_r.at[sent(i)], r_send.at[i])
-        left_sent(send_x.at[sent(i)], x_send.at[i])
-        return carry
-
-    lax.fori_loop(0, n_turn, drain, 0)
 
 
 def first_round(n_col, n_row, snapshots, orientation):

time: 58.5 us -> 57.9 us (0.990)
  Pallas kernels: 57.8 us -> 57.1 us
where the time goes in v4:
time: 57.9 us; the launch traced here: 57.7 us
  Pallas kernels  57.1 us (99%)
  between operations  0.64 us (1%)
    pallas_call x1, Pallas kernels, first_round(): pl.pallas_call(functools.partial(first_kernel, n_col, n_row), out_shape=[...  49.8 us
    pallas_call x1, Pallas kernels, last_round(): pl.pallas_call(functools.partial(last_kernel, n_col), out_shape=[jax.Shap...  7.3 us

profile of v4, /device:TPU:1, one launch (start us, length us, event | category | flops | bytes accessed | tf_op | source)
XLA Modules:
  0.0 57.7 jit_solution(4524474368190326224)
XLA Ops:
  0.6 49.8 %shard_map.41 = (f32[4096,128]{1,0:T(8,128)S(1)}, f32[4096,128]{1,0:T(8,128)S(1)}, f32[2,384,128]{2,1,0:T(8,128)S(1)}, f32[128,128]{1,0:T(8,128)S(1)}) custom-call(f32[4096,256]{1,0:T(8,128)} %x_ref.1, s32[2,8]{1,0:T(2,128)} %ori_ref.3), custom_call_target="tpu_custom_call" | custom-call | tf_op jit(solution)/shard_map/pallas_call | solution.py:431
  50.4 7.3 %shard_map.42 = (f32[4096,256]{1,0:T(8,128)}, f32[128,256]{1,0:T(8,128)}) custom-call(f32[4096,128]{1,0:T(8,128)S(1)} %get-tuple-element.6.u, f32[4096,128]{1,0:T(8,128)S(1)} %get-tuple-element.7.l, f32[2,384,128]{2,1,0:T(8,128)S(1)} %get-tuple-element.8.pack, f32[128,128]{1,0:T(8,128)S(1)} %get-tuple-element.9.c, s32[2,8]{1,0:T(2,128)} %ori_ref.3), custom_call_target="tpu_custom_call" | custom-call | tf_op jit(solution)/shard_map/pallas_call | solution.py:523
